TPU v7x, 32 devices: a whole 2x2x4 slice. The times are simulated.
32 devices in a mesh: dp: 8 (over z, x), mp: 4 (over y, core).
Axes of the slice: x: 2, y: 2, z: 4, core: 2. Of those that a mesh axis runs over, the one named last changes fastest.
Arguments:
- tokens: bfloat16 [16, 577, 1024], P('dp', None, 'mp'), may hold values from -32 to 32
- slot_flags: int32 [16], P('dp'), may hold values 0 or 1
- cotangent: bfloat16 [16, 577, 1024], P('dp', None, 'mp'), may hold values from -6 to 6
- attend_gain: bfloat16 [16, 64], P('mp', 'dp'), may hold values from 0.18 to 4.4
- attend_shift: bfloat16 [16, 64], P('mp', 'dp'), may hold values from -4 to 4
- input_weight: bfloat16 [1024, 3, 1024], P('dp', None, 'mp'), may hold values from -0.1875 to 0.1875
- input_bias: bfloat16 [2, 16, 64], P(None, 'mp', 'dp'), may hold values from -6 to 6
- output_weight: bfloat16 [1024, 1024], P('mp', 'dp'), may hold values from -0.5 to 0.5
- output_bias: bfloat16 [16, 64], P('mp', 'dp'), may hold values from -6 to 6
- dense_gain: bfloat16 [16, 64], P('mp', 'dp'), may hold values from 0.18 to 4.4
- dense_shift: bfloat16 [16, 64], P('mp', 'dp'), may hold values from -4 to 4
- up_weight: bfloat16 [1024, 4096], P('dp', 'mp'), may hold values from -0.1875 to 0.1875
- up_bias: bfloat16 [64, 64], P('mp', 'dp'), may hold values from -6 to 6
- down_weight: bfloat16 [4096, 1024], P('mp', 'dp'), may hold values from -0.09375 to 0.09375
- down_bias: bfloat16 [16, 64], P('mp', 'dp'), may hold values from -6 to 6
Outputs:
- layer_out: bfloat16 [16, 577, 1024], P('dp', None, 'mp')
- input_grad: float32 [16, 577, 1024], P('dp', None, 'mp')
- grad_attend_gain: float32 [16, 64], P('mp', 'dp')
- grad_attend_shift: float32 [16, 64], P('mp', 'dp')
- grad_input_weight: float32 [1024, 3, 1024], P('dp', None, 'mp')
- grad_input_bias: float32 [2, 16, 64], P(None, 'mp', 'dp')
- grad_output_weight: float32 [1024, 1024], P('mp', 'dp')
- grad_output_bias: float32 [16, 64], P('mp', 'dp')
- grad_dense_gain: float32 [16, 64], P('mp', 'dp')
- grad_dense_shift: float32 [16, 64], P('mp', 'dp')
- grad_up_weight: float32 [1024, 4096], P('dp', 'mp')
- grad_up_bias: float32 [64, 64], P('mp', 'dp')
- grad_down_weight: float32 [4096, 1024], P('mp', 'dp')
- grad_down_bias: float32 [16, 64], P('mp', 'dp')
Inputs may be any that keep to these rules, and one draw needn't show every extreme that they name: `slot_flags`: 1 marks a filled image slot, 0 an empty one.
All inputs are finite; a program needn't handle non-finite values. No bound on the sum of `slot_flags` on one device may be relied on, other than what follows from the above.
Results may differ from a plain program's by a relative error of at most 0.022.
Values may be sent and summed in bfloat16 or wider, within the bound.
A program may use at most 128 MiB of HBM per device.

v0:
```python
import jax
import jax.numpy as jnp
from jax import lax
from jax.sharding import PartitionSpec as P

HD = 64


EPS = 1e-06


def product(left_side, right_side):
    return jnp.dot(left_side, right_side, preferred_element_type=jnp.float32)


def product_inner(left_side, right_side):
    return lax.dot_general(
        left_side, right_side, (((0,), (0,)), ((), ())), preferred_element_type=jnp.float32
    )


def product_outer(left_side, right_side):
    return lax.dot_general(
        left_side, right_side, (((1,), (1,)), ((), ())), preferred_element_type=jnp.float32
    )


def exact_gelu(values):
    return jax.nn.gelu(values, approximate=False)


def normalize(values, norm_gain, norm_shift):
    model_width = values.shape[1] * lax.axis_size("mp")
    first_sum, second_sum = lax.psum(
        (jnp.sum(values, axis=1), jnp.sum(values * values, axis=1)), "mp"
    )
    center = first_sum / model_width
    inverse = lax.rsqrt(second_sum / model_width - center * center + EPS)
    scaled = (values - center[:, None]) * inverse[:, None]
    normed = (scaled * norm_gain + norm_shift).astype(jnp.bfloat16)
    return (scaled, inverse, lax.all_gather(normed, "mp", axis=1, tiled=True))


def normalize_back(grad_normed, scaled, inverse, norm_gain):
    model_width = grad_normed.shape[1] * lax.axis_size("mp")
    grad_scaled = grad_normed * norm_gain
    first_sum, second_sum = lax.psum(
        (jnp.sum(grad_scaled, axis=1), jnp.sum(grad_scaled * scaled, axis=1)), "mp"
    )
    grad_values = inverse[:, None] * (
        grad_scaled
        - first_sum[:, None] / model_width
        - scaled * (second_sum[:, None] / model_width)
    )
    return (grad_values, jnp.sum(grad_normed * scaled, axis=0), jnp.sum(grad_normed, axis=0))


def sum_branch(partial_rows):
    return lax.psum_scatter(
        partial_rows.astype(jnp.bfloat16), "mp", scatter_dimension=1, tiled=True
    ).astype(jnp.float32)


def spread_grads(partial_rows):
    return lax.psum_scatter(
        partial_rows.astype(jnp.bfloat16), "mp", scatter_dimension=1, tiled=True
    ).astype(jnp.float32)


def gather_grads(rows_low):
    return lax.all_gather(rows_low, "mp", axis=1, tiled=True)


def unpack(gathered):
    (
        attend_gain,
        attend_shift,
        input_weight,
        input_bias,
        output_weight,
        output_bias,
        dense_gain,
        dense_shift,
        up_weight,
        up_bias,
        down_weight,
        down_bias,
    ) = gathered
    width_heads = input_weight.shape[2]
    return (
        attend_gain.reshape(-1).astype(jnp.float32),
        attend_shift.reshape(-1).astype(jnp.float32),
        input_weight,
        input_bias.reshape(2, width_heads).astype(jnp.float32),
        output_weight,
        output_bias.reshape(-1).astype(jnp.float32),
        dense_gain.reshape(-1).astype(jnp.float32),
        dense_shift.reshape(-1).astype(jnp.float32),
        up_weight,
        up_bias.reshape(-1).astype(jnp.float32),
        down_weight,
        down_bias.reshape(-1).astype(jnp.float32),
    )


def forward_slot(token_rows, filled, prepared):
    (
        attend_gain,
        attend_shift,
        input_weight,
        input_bias,
        output_weight,
        output_bias,
        dense_gain,
        dense_shift,
        up_weight,
        up_bias,
        down_weight,
        down_bias,
    ) = prepared
    length = token_rows.shape[0]
    local_heads = input_weight.shape[2] // HD
    scaled_one, inverse_one, normed_one = normalize(token_rows, attend_gain, attend_shift)
    joint_rows = jnp.einsum(
        "sd,dtf->stf", normed_one, input_weight, preferred_element_type=jnp.float32
    )
    bias_full = jnp.stack([input_bias[0], jnp.zeros_like(input_bias[0]), input_bias[1]])
    joint_rows = (joint_rows + bias_full).astype(jnp.bfloat16).reshape(length, 3, local_heads, HD)
    queries = joint_rows[:, 0]
    key_rows = joint_rows[:, 1]
    values = joint_rows[:, 2]
    scores = jnp.einsum(
        "qhd,khd->hqk", queries, key_rows, preferred_element_type=jnp.float32
    ) * HD ** (-0.5)
    largest = jnp.max(scores, axis=-1, keepdims=True)
    exponent = jnp.exp(scores - largest)
    totals = jnp.sum(exponent, axis=-1, keepdims=True)
    soft_low = (exponent / totals).astype(jnp.bfloat16)
    log_totals = largest + jnp.log(totals)
    attended = jnp.einsum("hqk,khd->qhd", soft_low, values, preferred_element_type=jnp.float32)
    attended = attended.astype(jnp.bfloat16).reshape(length, local_heads * HD)
    hidden = token_rows + sum_branch(product(attended, output_weight)) + output_bias
    scaled_two, inverse_two, normed_two = normalize(hidden, dense_gain, dense_shift)
    pre_active = product(normed_two, up_weight) + up_bias
    active = exact_gelu(pre_active).astype(jnp.bfloat16)
    layer_out = filled * (hidden + sum_branch(product(active, down_weight)) + down_bias)
    stored = (
        scaled_one,
        inverse_one,
        normed_one,
        queries,
        key_rows,
        values,
        log_totals,
        attended,
        scaled_two,
        inverse_two,
        normed_two,
        pre_active,
        active,
    )
    return (layer_out, stored)


def backward_slot(slot_cotangent, filled, prepared, stored, shard_shapes):
    (
        attend_gain,
        attend_shift,
        input_weight,
        input_bias,
        output_weight,
        output_bias,
        dense_gain,
        dense_shift,
        up_weight,
        up_bias,
        down_weight,
        down_bias,
    ) = prepared
    (
        scaled_one,
        inverse_one,
        normed_one,
        queries,
        key_rows,
        values,
        log_totals,
        attended,
        scaled_two,
        inverse_two,
        normed_two,
        pre_active,
        active,
    ) = stored
    length = slot_cotangent.shape[0]
    local_heads = input_weight.shape[2] // HD
    grad_layer = filled * slot_cotangent.astype(jnp.float32)
    grad_feed = grad_layer.astype(jnp.bfloat16)
    grad_down_bias = jnp.sum(grad_feed.astype(jnp.float32), axis=0)
    feed_full = gather_grads(grad_feed)
    grad_down = product_inner(active, feed_full)
    grad_active = product_outer(feed_full, down_weight)
    unused, pullback = jax.vjp(exact_gelu, pre_active)
    (grad_pre,) = pullback(grad_active)
    grad_pre = grad_pre.astype(jnp.bfloat16)
    grad_up_bias = jnp.sum(grad_pre.astype(jnp.float32), axis=0)
    grad_up = product_inner(normed_two, grad_pre)
    grad_normed_two = spread_grads(product_outer(grad_pre, up_weight))
    grad_hidden_norm, grad_dense_gain, grad_dense_shift = normalize_back(
        grad_normed_two, scaled_two, inverse_two, dense_gain
    )
    grad_hidden = grad_layer + grad_hidden_norm
    grad_branch = grad_hidden.astype(jnp.bfloat16)
    grad_output_bias = jnp.sum(grad_branch.astype(jnp.float32), axis=0)
    branch_full = gather_grads(grad_branch)
    grad_output = product_inner(attended, branch_full)
    grad_attended = (
        product_outer(branch_full, output_weight)
        .astype(jnp.bfloat16)
        .reshape(length, local_heads, HD)
    )
    scores = jnp.einsum(
        "qhd,khd->hqk", queries, key_rows, preferred_element_type=jnp.float32
    ) * HD ** (-0.5)
    soft_weights = jnp.exp(scores - log_totals)
    soft_low = soft_weights.astype(jnp.bfloat16)
    grad_values = jnp.einsum(
        "hqk,qhd->khd", soft_low, grad_attended, preferred_element_type=jnp.float32
    )
    grad_soft = jnp.einsum(
        "qhd,khd->hqk", grad_attended, values, preferred_element_type=jnp.float32
    )
    grad_scores = soft_weights * (
        grad_soft - jnp.sum(grad_soft * soft_weights, axis=-1, keepdims=True)
    )
    grad_scores = grad_scores.astype(jnp.bfloat16)
    grad_queries = jnp.einsum(
        "hqk,khd->qhd", grad_scores, key_rows, preferred_element_type=jnp.float32
    ) * HD ** (-0.5)
    grad_keys = jnp.einsum(
        "hqk,qhd->khd", grad_scores, queries, preferred_element_type=jnp.float32
    ) * HD ** (-0.5)
    grad_joint = jnp.stack([grad_queries, grad_keys, grad_values], axis=1)
    grad_joint = grad_joint.astype(jnp.bfloat16).reshape(length, 3, local_heads * HD)
    joint_sums = jnp.sum(grad_joint.astype(jnp.float32), axis=0)
    grad_input_bias = jnp.stack([joint_sums[0], joint_sums[2]])
    grad_input = jnp.einsum(
        "sd,stf->dtf", normed_one, grad_joint, preferred_element_type=jnp.float32
    )
    grad_normed_one = spread_grads(
        jnp.einsum("stf,dtf->sd", grad_joint, input_weight, preferred_element_type=jnp.float32)
    )
    grad_tokens_norm, grad_attend_gain, grad_attend_shift = normalize_back(
        grad_normed_one, scaled_one, inverse_one, attend_gain
    )
    grad_tokens = grad_hidden + grad_tokens_norm
    gradients = (
        grad_attend_gain.reshape(shard_shapes[0]),
        grad_attend_shift.reshape(shard_shapes[1]),
        grad_input,
        grad_input_bias.reshape(shard_shapes[3]),
        grad_output,
        grad_output_bias.reshape(shard_shapes[5]),
        grad_dense_gain.reshape(shard_shapes[6]),
        grad_dense_shift.reshape(shard_shapes[7]),
        grad_up,
        grad_up_bias.reshape(shard_shapes[9]),
        grad_down,
        grad_down_bias.reshape(shard_shapes[11]),
    )
    return (grad_tokens, gradients)


def body(
    tokens,
    slot_flags,
    cotangent,
    attend_gain,
    attend_shift,
    input_weight,
    input_bias,
    output_weight,
    output_bias,
    dense_gain,
    dense_shift,
    up_weight,
    up_bias,
    down_weight,
    down_bias,
):
    shards = (
        attend_gain,
        attend_shift,
        input_weight,
        input_bias,
        output_weight,
        output_bias,
        dense_gain,
        dense_shift,
        up_weight,
        up_bias,
        down_weight,
        down_bias,
    )
    gather_dims = (1, 1, 0, 2, 1, 1, 1, 1, 0, 1, 1, 1)
    factor = lax.axis_size("dp")
    full_shapes = []
    for shard_now, dim_now in zip(shards, gather_dims):
        dims_list = list(shard_now.shape)
        dims_list[dim_now] = dims_list[dim_now] * factor
        full_shapes.append(tuple(dims_list))
    running = tuple((jnp.zeros(shape_now, jnp.float32) for shape_now in full_shapes))

    def slot_step(accumulated, record):
        slot_tokens, slot_cotangent, slot_flag = record
        filled = slot_flag.astype(jnp.float32)
        prepared = unpack(
            (
                lax.all_gather(attend_gain, "dp", axis=1, tiled=True),
                lax.all_gather(attend_shift, "dp", axis=1, tiled=True),
                lax.all_gather(input_weight, "dp", axis=0, tiled=True),
                lax.all_gather(input_bias, "dp", axis=2, tiled=True),
                lax.all_gather(output_weight, "dp", axis=1, tiled=True),
                lax.all_gather(output_bias, "dp", axis=1, tiled=True),
                lax.all_gather(dense_gain, "dp", axis=1, tiled=True),
                lax.all_gather(dense_shift, "dp", axis=1, tiled=True),
                lax.all_gather(up_weight, "dp", axis=0, tiled=True),
                lax.all_gather(up_bias, "dp", axis=1, tiled=True),
                lax.all_gather(down_weight, "dp", axis=1, tiled=True),
                lax.all_gather(down_bias, "dp", axis=1, tiled=True),
            )
        )
        layer_out, stored = forward_slot(slot_tokens.astype(jnp.float32), filled, prepared)
        prepared_back = unpack(
            (
                lax.all_gather(attend_gain, "dp", axis=1, tiled=True),
                lax.all_gather(attend_shift, "dp", axis=1, tiled=True),
                lax.all_gather(input_weight, "dp", axis=0, tiled=True),
                lax.all_gather(input_bias, "dp", axis=2, tiled=True),
                lax.all_gather(output_weight, "dp", axis=1, tiled=True),
                lax.all_gather(output_bias, "dp", axis=1, tiled=True),
                lax.all_gather(dense_gain, "dp", axis=1, tiled=True),
                lax.all_gather(dense_shift, "dp", axis=1, tiled=True),
                lax.all_gather(up_weight, "dp", axis=0, tiled=True),
                lax.all_gather(up_bias, "dp", axis=1, tiled=True),
                lax.all_gather(down_weight, "dp", axis=1, tiled=True),
                lax.all_gather(down_bias, "dp", axis=1, tiled=True),
            )
        )
        grad_tokens, gradients = backward_slot(
            slot_cotangent, filled, prepared_back, stored, full_shapes
        )
        accumulated = jax.tree.map(jnp.add, accumulated, gradients)
        return (accumulated, (layer_out.astype(jnp.bfloat16), grad_tokens))

    running, (layer_rows, input_grad) = lax.scan(
        slot_step, running, (tokens, cotangent, slot_flags)
    )
    finals = (
        lax.psum_scatter(
            running[0].astype(jnp.bfloat16), "dp", scatter_dimension=1, tiled=True
        ).astype(jnp.float32),
        lax.psum_scatter(
            running[1].astype(jnp.bfloat16), "dp", scatter_dimension=1, tiled=True
        ).astype(jnp.float32),
        lax.psum_scatter(
            running[2].astype(jnp.bfloat16), "dp", scatter_dimension=0, tiled=True
        ).astype(jnp.float32),
        lax.psum_scatter(
            running[3].astype(jnp.bfloat16), "dp", scatter_dimension=2, tiled=True
        ).astype(jnp.float32),
        lax.psum_scatter(
            running[4].astype(jnp.bfloat16), "dp", scatter_dimension=1, tiled=True
        ).astype(jnp.float32),
        lax.psum_scatter(
            running[5].astype(jnp.bfloat16), "dp", scatter_dimension=1, tiled=True
        ).astype(jnp.float32),
        lax.psum_scatter(
            running[6].astype(jnp.bfloat16), "dp", scatter_dimension=1, tiled=True
        ).astype(jnp.float32),
        lax.psum_scatter(
            running[7].astype(jnp.bfloat16), "dp", scatter_dimension=1, tiled=True
        ).astype(jnp.float32),
        lax.psum_scatter(
            running[8].astype(jnp.bfloat16), "dp", scatter_dimension=0, tiled=True
        ).astype(jnp.float32),
        lax.psum_scatter(
            running[9].astype(jnp.bfloat16), "dp", scatter_dimension=1, tiled=True
        ).astype(jnp.float32),
        lax.psum_scatter(
            running[10].astype(jnp.bfloat16), "dp", scatter_dimension=1, tiled=True
        ).astype(jnp.float32),
        lax.psum_scatter(
            running[11].astype(jnp.bfloat16), "dp", scatter_dimension=1, tiled=True
        ).astype(jnp.float32),
    )
    return (
        layer_rows,
        input_grad,
        finals[0],
        finals[1],
        finals[2],
        finals[3],
        finals[4],
        finals[5],
        finals[6],
        finals[7],
        finals[8],
        finals[9],
        finals[10],
        finals[11],
    )


def solution(mesh):
    return jax.shard_map(
        body,
        mesh=mesh,
        in_specs=(
            P("dp", None, "mp"),
            P("dp"),
            P("dp", None, "mp"),
            P("mp", "dp"),
            P("mp", "dp"),
            P("dp", None, "mp"),
            P(None, "mp", "dp"),
            P("mp", "dp"),
            P("mp", "dp"),
            P("mp", "dp"),
            P("mp", "dp"),
            P("dp", "mp"),
            P("mp", "dp"),
            P("mp", "dp"),
            P("mp", "dp"),
        ),
        out_specs=(
            P("dp", None, "mp"),
            P("dp", None, "mp"),
            P("mp", "dp"),
            P("mp", "dp"),
            P("dp", None, "mp"),
            P(None, "mp", "dp"),
            P("mp", "dp"),
            P("mp", "dp"),
            P("mp", "dp"),
            P("mp", "dp"),
            P("dp", "mp"),
            P("mp", "dp"),
            P("mp", "dp"),
            P("mp", "dp"),
        ),
        check_vma=False,
    )
```

profile of v0, /device:TPU:0, one launch (start us, length us, event | category | flops | bytes accessed | tf_op | source)
XLA Modules:
  0.0 1161.6 jit_solution(16223975622956247617)
XLA Ops:
  12.2 864.1 %while.37 = (s32[]{:T(128)}, f32[4,64]{1,0:T(4,128)S(1)}, f32[4,64]{1,0:T(4,128)S(1)}, f32[1024,3,256]{2,0,1:T(8,128)}, f32[2,4,64]{2,1,0:T(4,128)S(1)}, /*index...) while((s32[]{:T(128)}, f32[4,64]{1,0:T(4,128)S(1)}, ...), condition=%wide.region_32.33_spmd.clone, body=%wide.region_0.32_spmd.clone.sunk | while | flops 12020062208 | bytes 306889920 | solution.py:356
  12.6 22.2 %all-gather.22 = bf16[8,8,4]{1,2,0:T(4,128)(2,1)S(1)} all-gather(bf16[1,8,4]{1,2,0:T(4,128)(2,1)S(1)} %bitcast.334), channel_id=1, replica_groups=mesh['dp'=8,'mp'=4] {'dp'}, dimensions={0}, use_global_device_ids=true | all-gather | bytes 576 | tf_op jit(solution)/shard_map/while/body/eval_jaxpr/all_gather | solution.py:319
  35.0 16.3 %all-gather.21 = bf16[8,8,4]{1,2,0:T(4,128)(2,1)S(1)} all-gather(bf16[1,8,4]{1,2,0:T(4,128)(2,1)S(1)} %bitcast.335), channel_id=1, replica_groups=mesh['dp'=8,'mp'=4] {'dp'}, dimensions={0}, use_global_device_ids=true | all-gather | bytes 576 | tf_op jit(solution)/shard_map/while/body/eval_jaxpr/all_gather | solution.py:320
  51.5 5.7 all-reduce.17
  59.0 30.5 %all_gather.77 = bf16[2,4,64]{1,0,2:T(2,128)(2,1)S(1)} all-gather(bf16[2,4,8]{1,0,2:T(2,128)(2,1)S(1)} %get-tuple-element.986), channel_id=1, replica_groups=mesh['dp'=8,'mp'=4] {'dp'}, dimensions={2}, use_global_device_ids=true | all-gather | bytes 1152 | tf_op jit(solution)/shard_map/while/body/eval_jaxpr/all_gather | solution.py:322
  90.0 29.2 %all_gather.78 = bf16[256,1024]{1,0:T(8,128)(2,1)S(1)} all-gather(bf16[256,128]{1,0:T(8,128)(2,1)S(1)} %get-tuple-element.989), channel_id=1, replica_groups=mesh['dp'=8,'mp'=4] {'dp'}, dimensions={1}, use_global_device_ids=true | all-gather | bytes 589824 | tf_op jit(solution)/shard_map/while/body/eval_jaxpr/all_gather | solution.py:323
  119.3 5.9 all-gather.32.cloned.1.call-done
  136.9 18.7 %all-gather.20 = bf16[8,8,4]{1,2,0:T(4,128)(2,1)S(1)} all-gather(bf16[1,8,4]{1,2,0:T(4,128)(2,1)S(1)} %bitcast.336), channel_id=1, replica_groups=mesh['dp'=8,'mp'=4] {'dp'}, dimensions={0}, use_global_device_ids=true | all-gather | bytes 576 | tf_op jit(solution)/shard_map/while/body/eval_jaxpr/all_gather | solution.py:324
  155.8 16.3 %all-gather.19 = bf16[8,8,4]{1,2,0:T(4,128)(2,1)S(1)} all-gather(bf16[1,8,4]{1,2,0:T(4,128)(2,1)S(1)} %bitcast.337), channel_id=1, replica_groups=mesh['dp'=8,'mp'=4] {'dp'}, dimensions={0}, use_global_device_ids=true | all-gather | bytes 576 | tf_op jit(solution)/shard_map/while/body/eval_jaxpr/all_gather | solution.py:325
  172.2 18.3 %all-gather.18 = bf16[8,8,4]{1,2,0:T(4,128)(2,1)S(1)} all-gather(bf16[1,8,4]{1,2,0:T(4,128)(2,1)S(1)} %bitcast.338), channel_id=1, replica_groups=mesh['dp'=8,'mp'=4] {'dp'}, dimensions={0}, use_global_device_ids=true | all-gather | bytes 576 | tf_op jit(solution)/shard_map/while/body/eval_jaxpr/all_gather | solution.py:326
  191.9 6.2 all-reduce.18
  203.0 26.1 %all_gather.75 = bf16[16,64]{0,1:T(8,128)(2,1)S(1)} all-gather(bf16[16,8]{0,1:T(8,128)(2,1)S(1)} %get-tuple-element.994), channel_id=1, replica_groups=mesh['dp'=8,'mp'=4] {'dp'}, dimensions={1}, use_global_device_ids=true | all-gather | bytes 2304 | tf_op jit(solution)/shard_map/while/body/eval_jaxpr/all_gather | solution.py:328
  231.1 9.4 multiply_convert_fusion.5
  240.5 10.4 all-gather.40.cloned.1.call-done
  250.9 53.3 %all-gather.42.cloned.1.call-done = bf16[1024,1024]{1,0:T(8,128)(2,1)} async-done(((bf16[1024,128]{1,0:T(8,128)(2,1)}), bf16[1024,1024]{1,0:T(8,128)(2,1)}) %all-gather.42.cloned.1.call-update) | async-done | bytes 2097168 | tf_op jit(solution)/shard_map/while/body/eval_jaxpr/all_gather | solution.py:346
  304.2 5.7 convert_reduce_fusion.14
  313.7 24.1 %reduce-scatter.30.cloned.1.call-done = bf16[577,256]{1,0:T(8,128)(2,1)} async-done(((bf16[577,1024]{1,0:T(8,128)(2,1)}), bf16[577,256]{1,0:T(8,128)(2,1)}) %reduce-scatter.30.cloned.1.call-update) | async-done | bytes 295440 | tf_op jit(solution)/shard_map/while/body/eval_jaxpr/reduce_scatter | solution.py:65
  339.3 5.9 all-reduce.19
  347.5 20.8 %all-gather.23 = bf16[8,8,4]{1,2,0:T(4,128)(2,1)S(1)} all-gather(bf16[1,8,4]{1,2,0:T(4,128)(2,1)S(1)} %bitcast.339), channel_id=1, replica_groups=mesh['dp'=8,'mp'=4] {'dp'}, dimensions={0}, use_global_device_ids=true | all-gather | bytes 576 | tf_op jit(solution)/shard_map/while/body/eval_jaxpr/all_gather | solution.py:330
  368.6 4.1 convolution_convert_fusion.11
  372.7 5.2 select_add_fusion.27
  380.0 3.8 fusion.164
  384.8 4.6 multiply_reduce_fusion.8
  397.5 3.7 bitcast_convert_fusion.4
  401.2 5.2 select_add_fusion.25
  412.2 3.1 select_add_fusion.21
  415.3 9.2 reduce-scatter.32.cloned.1.call-done
  426.2 5.8 all-reduce.20
  434.1 9.2 dynamic_update_slice.14
  444.7 20.7 %all-gather.22 = bf16[8,8,4]{1,2,0:T(4,128)(2,1)S(1)} all-gather(bf16[1,8,4]{1,2,0:T(4,128)(2,1)S(1)} %bitcast.334), channel_id=1, replica_groups=mesh['dp'=8,'mp'=4] {'dp'}, dimensions={0}, use_global_device_ids=true | all-gather | bytes 576 | tf_op jit(solution)/shard_map/while/body/eval_jaxpr/all_gather | solution.py:319
  465.6 16.3 %all-gather.21 = bf16[8,8,4]{1,2,0:T(4,128)(2,1)S(1)} all-gather(bf16[1,8,4]{1,2,0:T(4,128)(2,1)S(1)} %bitcast.335), channel_id=1, replica_groups=mesh['dp'=8,'mp'=4] {'dp'}, dimensions={0}, use_global_device_ids=true | all-gather | bytes 576 | tf_op jit(solution)/shard_map/while/body/eval_jaxpr/all_gather | solution.py:320
  482.0 5.7 all-reduce.17
  489.5 30.5 %all_gather.77 = bf16[2,4,64]{1,0,2:T(2,128)(2,1)S(1)} all-gather(bf16[2,4,8]{1,0,2:T(2,128)(2,1)S(1)} %get-tuple-element.986), channel_id=1, replica_groups=mesh['dp'=8,'mp'=4] {'dp'}, dimensions={2}, use_global_device_ids=true | all-gather | bytes 1152 | tf_op jit(solution)/shard_map/while/body/eval_jaxpr/all_gather | solution.py:322
  520.6 29.3 %all_gather.78 = bf16[256,1024]{1,0:T(8,128)(2,1)S(1)} all-gather(bf16[256,128]{1,0:T(8,128)(2,1)S(1)} %get-tuple-element.989), channel_id=1, replica_groups=mesh['dp'=8,'mp'=4] {'dp'}, dimensions={1}, use_global_device_ids=true | all-gather | bytes 589824 | tf_op jit(solution)/shard_map/while/body/eval_jaxpr/all_gather | solution.py:323
  549.8 6.9 all-gather.32.cloned.1.call-done
  568.5 18.3 %all-gather.20 = bf16[8,8,4]{1,2,0:T(4,128)(2,1)S(1)} all-gather(bf16[1,8,4]{1,2,0:T(4,128)(2,1)S(1)} %bitcast.336), channel_id=1, replica_groups=mesh['dp'=8,'mp'=4] {'dp'}, dimensions={0}, use_global_device_ids=true | all-gather | bytes 576 | tf_op jit(solution)/shard_map/while/body/eval_jaxpr/all_gather | solution.py:324
  586.9 16.3 %all-gather.19 = bf16[8,8,4]{1,2,0:T(4,128)(2,1)S(1)} all-gather(bf16[1,8,4]{1,2,0:T(4,128)(2,1)S(1)} %bitcast.337), channel_id=1, replica_groups=mesh['dp'=8,'mp'=4] {'dp'}, dimensions={0}, use_global_device_ids=true | all-gather | bytes 576 | tf_op jit(solution)/shard_map/while/body/eval_jaxpr/all_gather | solution.py:325
  603.4 18.3 %all-gather.18 = bf16[8,8,4]{1,2,0:T(4,128)(2,1)S(1)} all-gather(bf16[1,8,4]{1,2,0:T(4,128)(2,1)S(1)} %bitcast.338), channel_id=1, replica_groups=mesh['dp'=8,'mp'=4] {'dp'}, dimensions={0}, use_global_device_ids=true | all-gather | bytes 576 | tf_op jit(solution)/shard_map/while/body/eval_jaxpr/all_gather | solution.py:326
  623.1 6.2 all-reduce.18
  633.9 26.1 %all_gather.75 = bf16[16,64]{0,1:T(8,128)(2,1)S(1)} all-gather(bf16[16,8]{0,1:T(8,128)(2,1)S(1)} %get-tuple-element.994), channel_id=1, replica_groups=mesh['dp'=8,'mp'=4] {'dp'}, dimensions={1}, use_global_device_ids=true | all-gather | bytes 2304 | tf_op jit(solution)/shard_map/while/body/eval_jaxpr/all_gather | solution.py:328
  662.2 9.4 multiply_convert_fusion.5
  671.6 10.4 all-gather.40.cloned.1.call-done
  682.0 53.2 %all-gather.42.cloned.1.call-done = bf16[1024,1024]{1,0:T(8,128)(2,1)} async-done(((bf16[1024,128]{1,0:T(8,128)(2,1)}), bf16[1024,1024]{1,0:T(8,128)(2,1)}) %all-gather.42.cloned.1.call-update) | async-done | bytes 2097168 | tf_op jit(solution)/shard_map/while/body/eval_jaxpr/all_gather | solution.py:346
  735.2 5.7 convert_reduce_fusion.14
  744.6 24.1 %reduce-scatter.30.cloned.1.call-done = bf16[577,256]{1,0:T(8,128)(2,1)} async-done(((bf16[577,1024]{1,0:T(8,128)(2,1)}), bf16[577,256]{1,0:T(8,128)(2,1)}) %reduce-scatter.30.cloned.1.call-update) | async-done | bytes 295440 | tf_op jit(solution)/shard_map/while/body/eval_jaxpr/reduce_scatter | solution.py:65
  770.2 5.9 all-reduce.19
  778.5 20.8 %all-gather.23 = bf16[8,8,4]{1,2,0:T(4,128)(2,1)S(1)} all-gather(bf16[1,8,4]{1,2,0:T(4,128)(2,1)S(1)} %bitcast.339), channel_id=1, replica_groups=mesh['dp'=8,'mp'=4] {'dp'}, dimensions={0}, use_global_device_ids=true | all-gather | bytes 576 | tf_op jit(solution)/shard_map/while/body/eval_jaxpr/all_gather | solution.py:330
  799.5 4.1 convolution_convert_fusion.11
  803.7 6.5 select_add_fusion.27
  812.2 3.8 fusion.164
  816.9 4.4 multiply_reduce_fusion.8
  829.4 3.7 bitcast_convert_fusion.4
  833.2 6.4 select_add_fusion.25
  845.4 5.6 select_add_fusion.21
  851.0 5.5 reduce-scatter.32.cloned.1.call-done
  858.2 5.8 all-reduce.20
  866.0 9.2 dynamic_update_slice.14
  878.7 3.2 convert_element_type.248
  887.1 3.9 convert_element_type.260
  894.6 37.4 %all-reduce.12 = (bf16[4,64]{1,0:T(4,128)(2,1)S(1)}, bf16[4,64]{1,0:T(4,128)(2,1)S(1)}, bf16[2,4,64]{2,1,0:T(4,128)(2,1)S(1)}, bf16[4,64]{1,0:T(4,128)(2,1)S(1)}...) all-reduce(bf16[4,64]{1,0:T(4,128)(2,1)S(1)} %convert_element_type., ...), channel_id=6, replica_groups=mesh['dp'=8,'mp'=4] {'dp'}, use_global_device_ids=true, to_apply=%region_33.34.clone | all-reduce | flops 3072 | bytes 12288
  935.2 8.7 reduce-scatter.24.cloned.1.call-done
  945.5 66.6 %reduce-scatter.20.cloned.1.call-done = bf16[128,3,256]{2,0,1:T(8,128)(2,1)} async-done(((bf16[1024,3,256]{2,0,1:T(8,128)(2,1)}), bf16[128,3,256]{2,0,1:T(8,128)(2,1)}) %reduce-scatter.20.cloned.1.call-update) | async-done | bytes 196624 | tf_op jit(solution)/shard_map/reduce_scatter | solution.py:366
  1013.8 68.2 %reduce-scatter.26.cloned.1.call-done = bf16[128,1024]{1,0:T(8,128)(2,1)} async-done(((bf16[1024,1024]{1,0:T(8,128)(2,1)}), bf16[128,1024]{1,0:T(8,128)(2,1)}) %reduce-scatter.26.cloned.1.call-update) | async-done | bytes 262160
  1084.0 68.3 %reduce-scatter.22.cloned.1.call-done = bf16[128,1024]{1,0:T(8,128)(2,1)} async-done(((bf16[1024,1024]{1,0:T(8,128)(2,1)}), bf16[128,1024]{1,0:T(8,128)(2,1)}) %reduce-scatter.22.cloned.1.call-update) | async-done | bytes 262160 | tf_op jit(solution)/shard_map/reduce_scatter | solution.py:384
  (373 shorter events, 128.0 us)
Async XLA Ops:
  8.0 4.1 copy-start.23
  8.0 4.1 copy-start.17
  8.0 4.1 copy-start.22
  8.0 4.1 copy-start.21
  8.1 4.1 copy-start.20
  8.1 4.1 copy-start.15
  8.1 4.1 copy-start.19
  8.1 4.1 copy-start.18
  8.1 4.1 copy-start.28
  12.2 107.1 %all-gather.34.cloned.1.call-start = ((), (), s32[]{:S(2)}) async-start(), calls=%async_computation.13 | async-start | bytes 1495040 | tf_op jit(solution)/shard_map/while/body/eval_jaxpr/all_gather | solution.py:41
  58.2 67.0 %all-gather.32.cloned.1.call-start = ((), (), s32[]{:S(2)}) async-start(), calls=%async_computation.12 | async-start | bytes 1769472 | tf_op jit(solution)/shard_map/while/body/eval_jaxpr/all_gather | solution.py:321
  58.9 131.8 %reduce-scatter.28.cloned.1.call-start = ((), (), s32[]{:S(2)}) async-start(), calls=%async_computation.14 | async-start | bytes 1495040 | tf_op jit(solution)/shard_map/while/body/eval_jaxpr/reduce_scatter | solution.py:59
  134.7 66.7 %copy-start.14 = (bf16[2,577,256]{2,1,0:T(8,128)(2,1)S(1)}, bf16[2,577,256]{2,1,0:T(8,128)(2,1)}, u32[]{:S(2)}) copy-start(bf16[2,577,256]{2,1,0:T(8,128)(2,1)} %get-tuple-element.988) | copy-start | bytes 1772548 | tf_op jit(solution)/shard_map/while
  136.3 92.9 %all-gather.38.cloned.1.call-start = ((), (), s32[]{:S(2)}) async-start(), calls=%async_computation.16 | async-start | bytes 2359296 | tf_op jit(solution)/shard_map/while/body/eval_jaxpr/all_gather | solution.py:327
  136.9 94.2 %all-gather.36.cloned.1.call-start = ((), (), s32[]{:S(2)}) async-start(), calls=%async_computation.15 | async-start | bytes 1495040 | tf_op jit(solution)/shard_map/while/body/eval_jaxpr/all_gather | solution.py:41
  200.1 50.8 %all-gather.40.cloned.1.call-start = ((), (), s32[]{:S(2)}) async-start(), calls=%async_computation.17 | async-start | bytes 1495040 | tf_op jit(solution)/shard_map/while/body/eval_jaxpr/all_gather | solution.py:71
  202.2 102.0 %all-gather.42.cloned.1.call-start = ((), (), s32[]{:S(2)}) async-start(), calls=%async_computation.18 | async-start | bytes 2359296 | tf_op jit(solution)/shard_map/while/body/eval_jaxpr/all_gather | solution.py:346
  202.9 134.9 %reduce-scatter.30.cloned.1.call-start = ((), (), s32[]{:S(2)}) async-start(), calls=%async_computation.19 | async-start | bytes 1495040 | tf_op jit(solution)/shard_map/while/body/eval_jaxpr/reduce_scatter | solution.py:65
  304.2 6.8 copy-start.24
  311.0 26.8 %copy-start.2 = (bf16[577,256]{1,0:T(8,128)(2,1)S(1)}, bf16[577,256]{1,0:T(8,128)(2,1)}, u32[]{:S(2)}) copy-start(bf16[577,256]{1,0:T(8,128)(2,1)} %reduce-scatter.28.cloned.1.call-done) | copy-start | bytes 886276 | tf_op jit(solution)/shard_map/while
  313.6 64.3 %all-gather.44.cloned.1.call-start = ((), (), s32[]{:S(2)}) async-start(), calls=%async_computation.20 | async-start | bytes 1495040 | tf_op jit(solution)/shard_map/while/body/eval_jaxpr/all_gather | solution.py:71
  347.5 59.3 %reduce-scatter.34.cloned.1.call-start = ((), (), s32[]{:S(2)}) async-start(), calls=%async_computation.22 | async-start | bytes 1495040 | tf_op jit(solution)/shard_map/while/body/eval_jaxpr/reduce_scatter | solution.py:59
  372.7 51.8 %reduce-scatter.32.cloned.1.call-start = ((), (), s32[]{:S(2)}) async-start(), calls=%async_computation.21 | async-start | bytes 1495040 | tf_op jit(solution)/shard_map/while/body/eval_jaxpr/reduce_scatter | solution.py:65
  383.9 5.5 slice-start
  384.7 4.6 slice-start.1
  394.4 3.0 copy-start.10
  397.4 3.7 copy-start.11
  397.5 3.8 copy-start.4
  406.4 3.6 copy-start.6
  406.4 3.6 copy-start.9
  408.7 3.5 copy-start.12
  412.2 3.1 copy-start.7
  412.2 19.9 %copy-start.5 = (f32[577,256]{1,0:T(8,128)S(1)}, f32[577,256]{1,0:T(8,128)}, u32[]{:S(2)}) copy-start(f32[577,256]{1,0:T(8,128)} %get-tuple-element.892) | copy-start | bytes 1772548 | tf_op jit(solution)/shard_map/while
  424.5 9.6 copy-start.26
  444.3 105.5 %all-gather.34.cloned.1.call-start = ((), (), s32[]{:S(2)}) async-start(), calls=%async_computation.13 | async-start | bytes 1495040 | tf_op jit(solution)/shard_map/while/body/eval_jaxpr/all_gather | solution.py:41
  488.7 68.0 %all-gather.32.cloned.1.call-start = ((), (), s32[]{:S(2)}) async-start(), calls=%async_computation.12 | async-start | bytes 1769472 | tf_op jit(solution)/shard_map/while/body/eval_jaxpr/all_gather | solution.py:321
  489.5 132.3 %reduce-scatter.28.cloned.1.call-start = ((), (), s32[]{:S(2)}) async-start(), calls=%async_computation.14 | async-start | bytes 1495040 | tf_op jit(solution)/shard_map/while/body/eval_jaxpr/reduce_scatter | solution.py:59
  561.5 2.6 copy-start
  566.2 66.3 %copy-start.14 = (bf16[2,577,256]{2,1,0:T(8,128)(2,1)S(1)}, bf16[2,577,256]{2,1,0:T(8,128)(2,1)}, u32[]{:S(2)}) copy-start(bf16[2,577,256]{2,1,0:T(8,128)(2,1)} %get-tuple-element.988) | copy-start | bytes 1772548 | tf_op jit(solution)/shard_map/while
  567.8 92.4 %all-gather.38.cloned.1.call-start = ((), (), s32[]{:S(2)}) async-start(), calls=%async_computation.16 | async-start | bytes 2359296 | tf_op jit(solution)/shard_map/while/body/eval_jaxpr/all_gather | solution.py:327
  568.4 93.8 %all-gather.36.cloned.1.call-start = ((), (), s32[]{:S(2)}) async-start(), calls=%async_computation.15 | async-start | bytes 1495040 | tf_op jit(solution)/shard_map/while/body/eval_jaxpr/all_gather | solution.py:41
  631.2 50.8 %all-gather.40.cloned.1.call-start = ((), (), s32[]{:S(2)}) async-start(), calls=%async_computation.17 | async-start | bytes 1495040 | tf_op jit(solution)/shard_map/while/body/eval_jaxpr/all_gather | solution.py:71
  633.3 101.9 %all-gather.42.cloned.1.call-start = ((), (), s32[]{:S(2)}) async-start(), calls=%async_computation.18 | async-start | bytes 2359296 | tf_op jit(solution)/shard_map/while/body/eval_jaxpr/all_gather | solution.py:346
  633.9 134.8 %reduce-scatter.30.cloned.1.call-start = ((), (), s32[]{:S(2)}) async-start(), calls=%async_computation.19 | async-start | bytes 1495040 | tf_op jit(solution)/shard_map/while/body/eval_jaxpr/reduce_scatter | solution.py:65
  735.2 6.8 copy-start.24
  742.0 26.8 %copy-start.2 = (bf16[577,256]{1,0:T(8,128)(2,1)S(1)}, bf16[577,256]{1,0:T(8,128)(2,1)}, u32[]{:S(2)}) copy-start(bf16[577,256]{1,0:T(8,128)(2,1)} %reduce-scatter.28.cloned.1.call-done) | copy-start | bytes 886276 | tf_op jit(solution)/shard_map/while
  744.6 65.6 %all-gather.44.cloned.1.call-start = ((), (), s32[]{:S(2)}) async-start(), calls=%async_computation.20 | async-start | bytes 1495040 | tf_op jit(solution)/shard_map/while/body/eval_jaxpr/all_gather | solution.py:71
  778.4 61.6 %reduce-scatter.34.cloned.1.call-start = ((), (), s32[]{:S(2)}) async-start(), calls=%async_computation.22 | async-start | bytes 1495040 | tf_op jit(solution)/shard_map/while/body/eval_jaxpr/reduce_scatter | solution.py:59
  803.6 52.8 %reduce-scatter.32.cloned.1.call-start = ((), (), s32[]{:S(2)}) async-start(), calls=%async_computation.21 | async-start | bytes 1495040 | tf_op jit(solution)/shard_map/while/body/eval_jaxpr/reduce_scatter | solution.py:65
  816.0 5.3 slice-start
  816.9 4.4 slice-start.1
  826.4 3.0 copy-start.10
  829.4 3.7 copy-start.11
  829.4 3.8 copy-start.4
  839.6 3.6 copy-start.6
  839.6 3.6 copy-start.9
  841.9 3.5 copy-start.12
  845.4 5.6 copy-start.7
  845.4 18.6 %copy-start.5 = (f32[577,256]{1,0:T(8,128)S(1)}, f32[577,256]{1,0:T(8,128)}, u32[]{:S(2)}) copy-start(f32[577,256]{1,0:T(8,128)} %get-tuple-element.892) | copy-start | bytes 1772548 | tf_op jit(solution)/shard_map/while
  856.4 9.6 copy-start.26
  876.3 67.6 %reduce-scatter.24.cloned.1.call-start = ((), (), s32[]{:S(2)}) async-start(), calls=%async_computation.10 | async-start | bytes 589824
  878.6 133.5 %reduce-scatter.20.cloned.1.call-start = ((), (), s32[]{:S(2)}) async-start(), calls=%async_computation.8 | async-start | bytes 1769472 | tf_op jit(solution)/shard_map/reduce_scatter | solution.py:366
  881.9 200.1 %reduce-scatter.26.cloned.1.call-start = ((), (), s32[]{:S(2)}) async-start(), calls=%async_computation.11 | async-start | bytes 2359296
  887.1 265.2 %reduce-scatter.22.cloned.1.call-start = ((), (), s32[]{:S(2)}) async-start(), calls=%async_computation.9 | async-start | bytes 2359296 | tf_op jit(solution)/shard_map/reduce_scatter | solution.py:384
  (15 other events, 23.7 us)
Sparse Core Ops, SparseCore 0:
  58.3 16.6 all-gather.33
  77.2 48.0 all-gather.31
  136.4 24.5 reduce-scatter.27
  163.2 49.4 all-gather.37
  214.8 16.2 all-gather.35
  233.2 17.6 all-gather.39
  253.1 51.0 all-gather.41
  313.8 24.0 reduce-scatter.29
  347.6 18.8 all-gather.43
  372.8 23.0 reduce-scatter.33
  401.3 23.0 reduce-scatter.31
  488.9 16.6 all-gather.33
  507.8 48.8 all-gather.31
  567.9 24.3 reduce-scatter.27
  594.5 49.3 all-gather.37
  645.9 16.2 all-gather.35
  664.3 17.6 all-gather.39
  684.1 51.0 all-gather.41
  744.7 23.9 reduce-scatter.29
  778.5 18.8 all-gather.43
  803.7 22.9 reduce-scatter.33
  833.3 23.0 reduce-scatter.31
Sparse Core Ops, SparseCore 1:
  880.7 63.2 reduce-scatter.23
  947.6 64.5 reduce-scatter.19
  1015.5 66.4 reduce-scatter.25
  1085.6 66.6 reduce-scatter.21
where the time goes:
time: 1160 us
  blocking collectives  480 us (41%)
  waiting for transfers between devices  423 us (36%)
  matrix products  131 us (11%)
  other arithmetic  54.6 us (5%)
  local copies, waits for them, and re-layouts  53.9 us (5%)
  between operations  16.7 us (1%)
    all_gather x2, waiting for transfers between devices, slot_step(): lax.all_gather(down_weight, 'dp', axis=1, tiled=True)  107 us
    unnamed x6, waiting for transfers between devices  76.9 us
    reduce_scatter x1, waiting for transfers between devices, body(): lax.psum_scatter(running[8].astype(jnp.bfloat16), 'dp', scatter_dimension...  68.3 us
    reduce_scatter x1, waiting for transfers between devices, body(): lax.psum_scatter(running[2].astype(jnp.bfloat16), 'dp', scatter_dimension...  66.6 us
    reduce_scatter x4, waiting for transfers between devices, spread_grads(): lax.psum_scatter(partial_rows.astype(jnp.bfloat16), 'mp', scatter_dimensi...  62.9 us
    all_gather x2, blocking collectives, slot_step(): lax.all_gather(input_bias, 'dp', axis=2, tiled=True)  61 us
    all_gather x2, blocking collectives, slot_step(): lax.all_gather(output_weight, 'dp', axis=1, tiled=True)  58.5 us
    all_gather x2, blocking collectives, slot_step(): lax.all_gather(up_bias, 'dp', axis=1, tiled=True)  52.2 us
  transfers between devices with their start and end apart: 26, of which 16 were waited for; matrix products, arithmetic and copies ran while one was open for 13% of the time, Pallas kernels for 0%

commit v1 on v0

v1 whole, which is shorter than its diff:
```python
import functools

import jax
import jax.numpy as jnp
from jax import lax
from jax.experimental import pallas as pl
from jax.experimental.pallas import tpu as pltpu
from jax.sharding import PartitionSpec as P

HD = 64
EPS = 1e-06
MESH = pl.DeviceIdType.MESH
BF = jnp.bfloat16
F32 = jnp.float32


def dot(left, right):
    return jnp.dot(left, right, preferred_element_type=F32)


def dot_nt(left, right):
    return lax.dot_general(left, right, (((1,), (1,)), ((), ())), preferred_element_type=F32)


def dot_tn(left, right):
    return lax.dot_general(left, right, (((0,), (0,)), ((), ())), preferred_element_type=F32)


class Ids:
    def __init__(self):
        self.count = 0

    def take(self, number):
        first = self.count
        self.count += number
        return first


class Sizes:
    def __init__(self, mesh, tokens, input_weight, up_weight):
        dp, mp = mesh.shape["dp"], mesh.shape["mp"]
        self.dp, self.mp = dp, mp
        self.A = 4 if dp % 4 == 0 else dp
        self.B = dp // self.A
        self.Y = mp // 2
        self.NS, self.SEQ, self.Dm = tokens.shape
        self.R = -(-self.SEQ // 32) * 32
        self.HR = self.R // 2
        self.ROWS = self.NS * self.R
        self.D = self.Dm * mp
        self.Dy = 2 * self.Dm
        self.RB = input_weight.shape[0]
        self.HW = input_weight.shape[2]
        self.NP = self.HW // 128
        self.F = up_weight.shape[1]
        self.VW = max(self.D, self.F, 2 * self.HW)
        self.cols = (3 * self.HW, self.HW, self.F, self.F)
        ids = Ids()
        A, B, Y, NS = self.A, self.B, self.Y, self.NS
        self.ag_r = [ids.take(A) for _ in range(4)]
        self.ag_l = [ids.take(A) for _ in range(4)]
        self.ag_x = [ids.take((B - 1) * A) for _ in range(4)]
        self.rs_r = [ids.take(A) for _ in range(4)]
        self.rs_l = [ids.take(A) for _ in range(4)]
        self.rs_x = [ids.take((B - 1) * A) for _ in range(4)]
        self.rows_c = [ids.take(1) for _ in range(2)]
        self.rows_y = [ids.take(Y) for _ in range(2)]
        self.rows_f = [ids.take(Y) for _ in range(2)]
        self.vec_ids = [[ids.take(n) for n in (A, B, 1, Y)] for _ in range(2)]
        self.slot_core = {
            name: [ids.take(1) for _ in range(NS)]
            for name in ("branch", "n2", "out", "lo", "gn2", "gb", "gn1", "ig")
        }
        self.slot_y = {
            name: [ids.take(Y) for _ in range(NS)] for name in ("branch", "out", "gn2", "gn1", "st")
        }
        self.local = ids.take(16)
        self.nsem = ids.count


SCRATCH = (
    "tokF", "feedF", "W0", "W1", "W2", "W3", "na", "q", "k", "v", "att", "csend", "cr1", "ysend", "yr1",
    "yrO", "hid", "n2", "gp", "cr2", "yr2", "gb", "gatt", "gj", "cr3", "yr3", "ebuf", "obuf", "stat", "statT",
    "statR", "ubuf", "lse", "G0", "G1", "G2", "G3", "RX0", "RX1", "RX2", "RX3", "ZL0", "ZL1", "ZL2", "ZL3",
    "ZR0", "ZR1", "ZR2", "ZR3", "vst", "vrA", "vrB", "vrC", "vrY", "acc", "gvl", "ss", "rs",
)
OPERANDS = (
    "tok", "feed", "w0", "w1", "w2", "w3", "vec", "lo", "ig", "o0", "o1", "o2", "o3", "gvec",
)


def scratch_shapes(z):
    A, B, Y, NS = z.A, z.B, z.Y, z.NS
    V = pltpu.VMEM
    half = (NS, z.HR, z.D)
    shapes = dict(
        tokF=V((z.ROWS, z.D), BF),
        feedF=V((z.ROWS, z.D), BF),
        na=V((z.ROWS, max(z.D, z.F)), BF),
        q=V((z.ROWS, z.HW), BF),
        k=V((z.ROWS, z.HW), BF),
        v=V((z.ROWS, z.HW), BF),
        att=V((z.ROWS, z.HW), BF),
        csend=V(half, BF),
        cr1=V(half, BF),
        ysend=V(half, BF),
        yr1=V((NS, Y - 1, z.HR, z.D), BF),
        yrO=V((NS, Y - 1, z.HR, z.Dy), BF),
        hid=V((NS * z.HR, z.D), F32),
        n2=V((z.ROWS, z.D), BF),
        gp=V((z.ROWS, z.F), BF),
        cr2=V(half, BF),
        yr2=V((NS, Y - 1, z.HR, z.D), BF),
        gb=V((z.ROWS, z.D), BF),
        gatt=V((z.R, z.HW), BF),
        gj=V((z.ROWS, 3 * z.HW), BF),
        cr3=V(half, BF),
        yr3=V((NS, Y - 1, z.HR, z.Dy), BF),
        ebuf=V((NS, z.HR, z.Dy), F32),
        obuf=V((NS, z.HR, z.Dy), BF),
        stat=V((z.HR, 128), F32),
        statT=V((NS, 8, z.HR), F32),
        statR=V((NS, Y - 1, 8, z.HR), F32),
        ubuf=V((z.R, min(512, z.F)), F32),
        lse=V((NS * 2 * z.NP, 1, z.R), F32),
        vst=V((2, 5, 8, z.VW), F32),
        vrA=V((2, A, 8, z.VW), F32),
        vrB=V((2, B, 8, z.VW), F32),
        vrC=V((2, 1, 8, z.VW), F32),
        vrY=V((2, Y, 8, z.VW), F32),
        acc=V((3, 8, z.D), F32),
        gvl=V((8, z.VW), F32),
        ss=pltpu.SemaphoreType.DMA((z.nsem,)),
        rs=pltpu.SemaphoreType.DMA((z.nsem,)),
    )
    for p, cols in enumerate(z.cols):
        shapes[f"W{p}"] = V((z.D, cols), BF)
        shapes[f"G{p}"] = V((z.D, cols), BF)
        shapes[f"RX{p}"] = V((max(B - 1, 1), A, z.RB, cols), BF)
        shapes[f"ZL{p}"] = V((A - 1, z.RB, cols), BF)
        shapes[f"ZR{p}"] = V((A - 1, z.RB, cols), BF)
    return [shapes[name] for name in SCRATCH]


def kernel(z, *refs):
    r = dict(zip(OPERANDS + SCRATCH, refs))
    A, B, Y, NS, R, HR, D, Dm, Dy, HW, F, RB = (
        z.A, z.B, z.Y, z.NS, z.R, z.HR, z.D, z.Dm, z.Dy, z.HW, z.F, z.RB,
    )
    ss, rs = r["ss"], r["rs"]
    dpi, mpi = lax.axis_index("dp"), lax.axis_index("mp")
    a, b = dpi // B, dpi % B
    y, c = mpi // 2, mpi % 2

    def dev(a=a, b=b, y=y, c=c):
        return (a * B + b, y * 2 + c)

    def rcopy(src, dst, i, device):
        return pltpu.make_async_remote_copy(
            src_ref=src, dst_ref=dst, send_sem=ss.at[i], recv_sem=rs.at[i],
            device_id=device, device_id_type=MESH,
        )

    def when(cond, f):
        if cond is True:
            f()
        elif cond is not False:
            pl.when(cond)(f)

    pending = []

    def send(copy, cond=True, late=True):
        when(cond, lambda: copy.start())
        if late:
            pending.append((cond, copy))
        return copy

    mate = dev(c=1 - c)

    def y_dev(dy):
        return dev(y=lax.rem(y + dy, Y))

    def b_dev(db):
        return dev(b=lax.rem(b + db, B))

    def a_dev(da):
        return dev(a=lax.rem(a + da, A))

    left, right = dev(a=jnp.maximum(a - 1, 0)), dev(a=jnp.minimum(a + 1, A - 1))

    def rows16(start, size):
        return pl.ds(pl.multiple_of(start, 16), size)

    def lanes(start, size):
        return pl.ds(pl.multiple_of(start, 128), size)

    def loop(n, f, unroll=1):
        def step(i, carry):
            f(i)
            return carry
        lax.fori_loop(0, n, step, 0, unroll=unroll)

    bar = pltpu.get_barrier_semaphore()
    friends = [mate] + [y_dev(i) for i in range(1, Y)] + [b_dev(i) for i in range(1, B)]
    friends += [a_dev(i) for i in range(1, A)]
    for friend in friends:
        pl.semaphore_signal(bar, inc=1, device_id=friend, device_id_type=MESH)
    pl.semaphore_wait(bar, len(friends))

    W = [r[f"W{p}"] for p in range(4)]
    wsh = [r[f"w{p}"] for p in range(4)]

    def wblock(p, blk):
        return W[p].at[rows16(blk * RB, RB)]

    def ag_out(p, src, blk_a, hop, go_right, go_left):
        blk = blk_a * B + b
        dst = wblock(p, blk)
        send(rcopy(src, dst, z.ag_r[p] + hop, right), go_right)
        send(rcopy(src, dst, z.ag_l[p] + hop, left), go_left)

    def ag_cross(p, src, blk_a, cond):
        dst = wblock(p, blk_a * B + b)
        for db in range(1, B):
            send(rcopy(src, dst, z.ag_x[p] + (db - 1) * A + blk_a, b_dev(db)), cond)

    def ag_start(p):
        own = wblock(p, dpi)
        local = pltpu.make_async_copy(wsh[p], own, ss.at[z.local + p])
        local.start()
        ag_out(p, wsh[p], a, 1, a < A - 1, a > 0)
        ag_cross(p, wsh[p], a, True)
        return local

    def ag_step(p, h):
        from_left = a >= h
        src_a = jnp.maximum(a - h, 0)
        src = wblock(p, src_a * B + b)

        def got_left():
            rcopy(src, src, z.ag_r[p] + h, right).wait_recv()
        when(from_left, got_left)
        if h < A - 1:
            send(rcopy(src, src, z.ag_r[p] + h + 1, right), from_left & (a < A - 1))
        ag_cross(p, src, src_a, from_left)
        from_right = a + h < A
        src_a2 = jnp.minimum(a + h, A - 1)
        src2 = wblock(p, src_a2 * B + b)

        def got_right():
            rcopy(src2, src2, z.ag_l[p] + h, left).wait_recv()
        when(from_right, got_right)
        if h < A - 1:
            send(rcopy(src2, src2, z.ag_l[p] + h + 1, left), from_right & (a > 0))
        ag_cross(p, src2, src_a2, from_right)

    def ag_done(p):
        for db in range(1, B):
            bs = lax.rem(b + B - db, B)
            for aa in range(A):
                blk = wblock(p, aa * B + bs)
                rcopy(blk, blk, z.ag_x[p] + (db - 1) * A + aa, mate).wait_recv()

    full = [r["tokF"], r["feedF"]]
    own_rows = [r["tok"], r["feed"]]

    def mblock(t, m):
        return full[t].at[:, lanes(m * Dm, Dm)]

    def rows_start(t):
        src = own_rows[t]
        local = pltpu.make_async_copy(src, mblock(t, mpi), ss.at[z.local + 4 + t])
        local.start()
        for dy in range(1, Y):
            send(rcopy(src, mblock(t, mpi), z.rows_y[t] + dy, y_dev(dy)))
        send(rcopy(src, mblock(t, mpi), z.rows_c[t], mate))
        return local

    def rows_relay(t):
        for dy in range(1, Y):
            blk = mblock(t, lax.rem(y + Y - dy, Y) * 2 + c)
            rcopy(blk, blk, z.rows_y[t] + dy, mate).wait_recv()
            send(rcopy(blk, blk, z.rows_f[t] + dy, mate))

    def rows_done(t):
        blk = mblock(t, y * 2 + 1 - c)
        rcopy(blk, blk, z.rows_c[t], mate).wait_recv()
        for dy in range(1, Y):
            blk = mblock(t, lax.rem(y + Y - dy, Y) * 2 + 1 - c)
            rcopy(blk, blk, z.rows_f[t] + dy, mate).wait_recv()

    vst = r["vst"]
    vr = (r["vrA"], r["vrB"], r["vrC"], r["vrY"])
    groups = (A, B, 2, Y)

    def vec_peer(stage, d):
        return (a_dev, b_dev, lambda _: mate, y_dev)[stage](d)

    def vec_send(use, stage):
        for d in range(1, groups[stage]):
            slot = d - 1
            send(rcopy(vst.at[use, stage], vr[stage].at[use, slot], z.vec_ids[use][stage] + slot, vec_peer(stage, d)))

    def vec_add(use, stage):
        total = vst[use, stage]
        for d in range(1, groups[stage]):
            slot = d - 1
            dst = vr[stage].at[use, slot]
            rcopy(dst, dst, z.vec_ids[use][stage] + slot, mate).wait_recv()
            got = vr[stage][use, slot]
            if stage >= 2:
                got = jnp.where(lax.broadcasted_iota(jnp.int32, got.shape, 0) < 6, got, 0.0)
            total = total + got
        vst[use, stage + 1] = total

    def vector(row, cols=slice(None)):
        return vst[0, 4, row:row + 1, cols]

    waits = [rows_start(0), ag_start(0), ag_start(1)]
    vst[0, 0] = r["vec"][...]
    vec_send(0, 0)
    vec_add(0, 0)
    vec_send(0, 1)
    ag_step(0, 1)
    vec_add(0, 1)
    vec_send(0, 2)
    vec_add(0, 2)
    vec_send(0, 3)
    if A > 2:
        ag_step(0, 2)
    vec_add(0, 3)
    waits.append(ag_start(2))
    rows_relay(0)
    waits.append(rows_start(1))
    rows_done(0)
    waits.append(ag_start(3))
    for h in range(3, A):
        ag_step(0, h)
    for w in waits:
        w.wait()

    tokF, feedF, na, n2 = r["tokF"], r["feedF"], r["na"], r["n2"]

    def stats(x):
        mu = jnp.sum(x, axis=1, keepdims=True) * (1.0 / D)
        sq = jnp.sum(x * x, axis=1, keepdims=True) * (1.0 / D)
        return mu, lax.rsqrt(sq - mu * mu + EPS)

    def norm_one():
        gain, shift = vector(0, slice(0, D)), vector(1, slice(0, D))

        def step(i):
            rr = rows16(i * 32, 32)
            x = tokF[rr, :].astype(F32)
            mu, inv = stats(x)
            na[rr, :D] = ((x - mu) * inv * gain + shift).astype(BF)
        loop(z.ROWS // 32, step)

    norm_one()
    ag_done(0)

    ticks = []
    for p in (1, 2, 3):
        for h in range(1, A):
            ticks.append(functools.partial(ag_step, p, h))
        ticks.append(functools.partial(ag_done, p))

    def tick(n=1):
        for _ in range(n):
            if ticks:
                ticks.pop(0)()

    q, k, v, att, lse = r["q"], r["k"], r["v"], r["att"], r["lse"]

    def project(s):
        rr = slice(s * R, s * R + R)
        x = na[rr, :D]
        for third, ref in enumerate((q, k, v)):
            for j in range(0, HW, 256):
                w = min(256, HW - j)
                col = third * HW + j
                out = dot(x, W[0][:, col:col + w])
                if third == 0:
                    out = out + vst[0, 4, 7:8, j:j + w]
                if third == 2:
                    out = out + vst[0, 4, 7:8, HW + j:HW + j + w]
                out = out.astype(BF)
                if third == 0:
                    out = out * BF(HD ** -0.5)
                ref[rr, j:j + w] = out

    chunks = [(i, min(256, R - i)) for i in range(0, R, 256)]
    top = z.SEQ // 16 * 16

    def half_mask(x, e):
        lane = lax.broadcasted_iota(jnp.int32, x.shape, 1)
        return jnp.where((lane < HD) if e == 0 else (lane >= HD), x, jnp.zeros_like(x))

    def mask_keys(scores):
        row = lax.broadcasted_iota(jnp.int32, scores.shape, 0)
        return jnp.where(row < z.SEQ, scores, -1e30)

    def attend(s, pr):
        cc = lanes(pr * 128, 128)
        rr = slice(s * R, s * R + R)
        kp = k[rr, cc]
        vt = v[rr, cc].T
        for (c0, cw) in chunks:
            qp = q[s * R + c0:s * R + c0 + cw, cc]
            parts = []
            for e in range(2):
                sc = mask_keys(dot_nt(kp, half_mask(qp, e)))
                mx = jnp.max(sc, axis=0, keepdims=True)
                ex = jnp.exp(sc - mx)
                tot = jnp.sum(ex, axis=0, keepdims=True)
                soft = (ex * (1.0 / tot)).astype(BF)
                parts.append(dot(vt[e * HD:(e + 1) * HD], soft))
                lse[(s * z.NP + pr) * 2 + e, :, c0:c0 + cw] = mx + jnp.log(tot)
            out = jnp.concatenate(parts, axis=0)
            att[s * R + c0:s * R + c0 + cw, cc] = out.T.astype(BF)

    csend, ysend = r["csend"], r["ysend"]
    busy = {}

    def free(key):
        for copy in busy.pop(key, []):
            copy.wait_send()

    def own(s):
        return rows16(s * R + c * HR, HR)

    def theirs(s):
        return rows16(s * R + (1 - c) * HR, HR)

    def core_part(s, name, x, w, dst):
        free(("c", s))
        rows_x = x[theirs(s), :]

        def step(j):
            cols = lanes(j * 256, 256)
            csend[s, :, cols] = dot_nt(rows_x, w[pl.ds(pl.multiple_of(j * 256, 256), 256), :]).astype(BF)
        loop(D // 256, step)
        copy = rcopy(csend.at[s], dst.at[s], z.slot_core[name][s], mate)
        busy[("c", s)] = [send(copy, late=False)]

    def core_wait(s, name, dst):
        rcopy(dst.at[s], dst.at[s], z.slot_core[name][s], mate).wait_recv()

    def chip_part(s, name, x, w, got, dst):
        core_wait(s, name, got)
        free(("y", s))
        rows_x = x[own(s), :]

        def step(j):
            cols = lanes(j * 256, 256)
            part = dot_nt(rows_x, w[pl.ds(pl.multiple_of(j * 256, 256), 256), :])
            ysend[s, :, cols] = (part + got[s, :, cols].astype(F32)).astype(BF)
        loop(D // 256, step)
        busy[("y", s)] = [
            send(rcopy(ysend.at[s], dst.at[s, dy - 1], z.slot_y[name][s] + dy - 1, y_dev(dy)), late=False)
            for dy in range(1, Y)
        ]

    def chip_share(s, name, x, w, got, dst):
        core_wait(s, name, got)
        free(("y", s))
        rows_x = x[own(s), :]
        copies = []
        for dy in range(1, Y):
            first = lax.rem(y + dy, Y) * Dy
            part = dot_nt(rows_x, w[rows16(first, Dy), :]) + got[s, :, lanes(first, Dy)].astype(F32)
            span = slice((dy - 1) * Dy, dy * Dy)
            ysend[s, :, span] = part.astype(BF)
            copies.append(send(rcopy(
                ysend.at[s, :, span], dst.at[s, dy - 1], z.slot_y[name][s] + dy - 1, y_dev(dy)
            ), late=False))
        busy[("y", s)] = copies

    def y_wait(s, name, dst):
        for dy in range(1, Y):
            got = dst.at[s, dy - 1]
            rcopy(got, got, z.slot_y[name][s] + dy - 1, mate).wait_recv()

    def own_share(s, x, w, got, dst):
        first = y * Dy
        total = dot_nt(x[own(s), :], w[rows16(first, Dy), :]) + got[s, :, lanes(first, Dy)].astype(F32)
        for dy in range(1, Y):
            total = total + dst[s, dy - 1].astype(F32)
        return total

    hid = r["hid"]
    cr1, cr2, cr3, yr1, yr2, yr3, yrO = (r[n] for n in ("cr1", "cr2", "cr3", "yr1", "yr2", "yr3", "yrO"))

    def norm_two(s):
        y_wait(s, "branch", yr1)
        gain, shift, bias = vector(3, slice(0, D)), vector(4, slice(0, D)), vector(2, slice(0, D))

        def step(i):
            lr = rows16(i * 16, 16)
            h = ysend[s, lr, :].astype(F32)
            for dy in range(Y - 1):
                h = h + yr1[s, dy, lr, :].astype(F32)
            gr = rows16(s * R + c * HR + i * 16, 16)
            h = tokF[gr, :].astype(F32) + (h + bias)
            hid[rows16(s * HR + i * 16, 16), :] = h
            mu, inv = stats(h)
            n2[gr, :] = ((h - mu) * inv * gain + shift).astype(BF)
        loop(HR // 16, step)
        part = n2.at[own(s)]
        send(rcopy(part, part, z.slot_core["n2"][s], mate))
        yc = lanes(y * Dy, Dy)
        ebuf[s] = hid[s * HR:s * HR + HR, yc] + vst[0, 4, 5:6, yc]

    ubuf, gp = r["ubuf"], r["gp"]
    UC = min(512, F)
    root = 0.5 ** 0.5
    dens = (2.0 * 3.141592653589793) ** -0.5

    def up(s):
        part = n2.at[theirs(s)]
        rcopy(part, part, z.slot_core["n2"][s], mate).wait_recv()
        x = n2[s * R:s * R + R, :]

        def column(j):
            cols = lanes(j * UC, UC)
            ubuf[...] = dot(x, W[2][:, cols]) + vst[0, 4, 6:7, cols]

            def step(i):
                lr = rows16(i * 32, 32)
                gr = rows16(s * R + i * 32, 32)
                u = ubuf[lr, :]
                phi = 0.5 * lax.erf(u * root) + 0.5
                na[gr, cols] = (u * phi).astype(BF)
                gp[gr, cols] = (phi + u * (jnp.exp(-0.5 * u * u) * dens)).astype(BF)
            loop(R // 32, step)
        loop(F // UC, column)

    def back_up(s):
        x = feedF[s * R:s * R + R, :]

        def column(j):
            cols = lanes(j * 256, 256)
            ga = dot(x, W[3][:, cols])
            gp[s * R:s * R + R, cols] = (ga * gp[s * R:s * R + R, cols].astype(F32)).astype(BF)
        loop(F // 256, column)

    obuf, ebuf, lo, ig = r["obuf"], r["ebuf"], r["lo"], r["ig"]

    def layer_out(s):
        y_wait(s, "out", yrO)
        total = own_share(s, na_act, W[3], cr1, yrO)
        obuf[s] = (total + ebuf[s]).astype(BF)
        give_out(s, obuf, lo, "lo")

    def give_out(s, buf, out, name):
        out[own(s), :] = buf[s, :, lanes(c * Dm, Dm)]
        send(rcopy(buf.at[s, :, lanes((1 - c) * Dm, Dm)], out.at[own(s)], z.slot_core[name][s], mate))

    def take_out(s, out, name):
        dst = out.at[theirs(s)]
        rcopy(dst, dst, z.slot_core[name][s], mate).wait_recv()

    na_act = na.at[:, 0:F]
    gb, gatt, gj, acc, gvl = r["gb"], r["gatt"], r["gj"], r["acc"], r["gvl"]

    def norm_two_back(s):
        y_wait(s, "gn2", yr2)
        gain = vector(3, slice(0, D))

        def step(i, sums):
            lr = rows16(i * 16, 16)
            e = ysend[s, lr, :].astype(F32)
            for dy in range(Y - 1):
                e = e + yr2[s, dy, lr, :].astype(F32)
            hr = rows16(s * HR + i * 16, 16)
            gr = rows16(s * R + c * HR + i * 16, 16)
            h = hid[hr, :]
            mu, inv = stats(h)
            xhat = (h - mu) * inv
            t = e * gain
            m1 = jnp.sum(t, axis=1, keepdims=True) * (1.0 / D)
            m2 = jnp.sum(t * xhat, axis=1, keepdims=True) * (1.0 / D)
            g = feedF[gr, :].astype(F32) + inv * (t - m1 - xhat * m2)
            hid[hr, :] = g
            g = g.astype(BF)
            gb[gr, :] = g
            g = g.astype(F32)
            ex = e * xhat
            fold = lambda m: m[0:8] + m[8:16]
            return (sums[0] + fold(ex), sums[1] + fold(e), sums[2] + fold(g))
        zero = jnp.zeros((8, D), F32)
        sums = lax.fori_loop(0, HR // 16, step, (zero, zero, zero))
        for i in range(3):
            acc[i] = sums[i] if s == 0 else acc[i] + sums[i]
        part = gb.at[own(s)]
        send(rcopy(part, part, z.slot_core["gb"][s], mate))

    def attend_back_start(s):
        part = gb.at[theirs(s)]
        rcopy(part, part, z.slot_core["gb"][s], mate).wait_recv()
        gatt[...] = dot(gb[s * R:s * R + R, :], W[1][...]).astype(BF)

    def attend_back(s, pr):
        cc = lanes(pr * 128, 128)
        rr = slice(s * R, s * R + R)
        kp = k[rr, cc]
        vp = v[rr, cc]
        kt = kp.T
        dk = jnp.zeros((R, 128), F32)
        dv = jnp.zeros((R, 128), F32)
        for (c0, cw) in chunks:
            qp = q[s * R + c0:s * R + c0 + cw, cc]
            go = gatt[c0:c0 + cw, cc]
            parts = []
            for e in range(2):
                qm, gm = half_mask(qp, e), half_mask(go, e)
                sc = mask_keys(dot_nt(kp, qm))
                soft = jnp.exp(sc - lse[(s * z.NP + pr) * 2 + e, :, c0:c0 + cw])
                dv = dv + dot(soft.astype(BF), gm)
                gs = dot_nt(vp, gm)
                delta = jnp.sum(gs * soft, axis=0, keepdims=True)
                ds = (soft * (gs - delta)).astype(BF)
                dk = dk + dot(ds, qm)
                parts.append(dot(kt[e * HD:(e + 1) * HD], ds))
            dq = jnp.concatenate(parts, axis=0) * (HD ** -0.5)
            gj[s * R + c0:s * R + c0 + cw, lanes(pr * 128, 128)] = dq.T.astype(BF)
        gj[rr, lanes(HW + pr * 128, 128)] = dk.astype(BF)
        gj[rr, lanes(2 * HW + pr * 128, 128)] = dv.astype(BF)

    stat, statT, statR = r["stat"], r["statT"], r["statR"]

    def norm_one_sums(s):
        y_wait(s, "gn1", yr3)
        ebuf[s] = own_share(s, gj, W[0], cr3, yr3)
        yc = lanes(y * Dy, Dy)
        gain = vector(0, yc)

        def step(i, sums):
            lr = rows16(i * 16, 16)
            gr = rows16(s * R + c * HR + i * 16, 16)
            mu, inv = stats(tokF[gr, :].astype(F32))
            xhat = (tokF[gr, yc].astype(F32) - mu) * inv
            e = ebuf[s, lr, :]
            t = e * gain
            s1 = jnp.sum(t, axis=1, keepdims=True)
            s2 = jnp.sum(t * xhat, axis=1, keepdims=True)
            lane = lax.broadcasted_iota(jnp.int32, (16, 128), 1)
            stat[lr, :] = jnp.where(lane == 0, s1, jnp.where(lane == 1, s2, 0.0))
            ex = e * xhat
            fold = lambda m: m[0:8] + m[8:16]
            return (sums[0] + fold(ex), sums[1] + fold(e))
        zero = jnp.zeros((8, Dy), F32)
        sums = lax.fori_loop(0, HR // 16, step, (zero, zero))
        for i in range(2):
            row = jnp.sum(sums[i], axis=0, keepdims=True)
            gvl[i:i + 1, yc] = row if s == 0 else gvl[i:i + 1, yc] + row
        statT[s] = stat[...].T[0:8]
        for dy in range(1, Y):
            send(rcopy(statT.at[s], statR.at[s, dy - 1], z.slot_y["st"][s] + dy - 1, y_dev(dy)))

    def norm_one_back(s):
        y_wait(s, "st", statR)
        total = statT[s]
        for dy in range(Y - 1):
            total = total + statR[s, dy]
        total = jnp.concatenate([total, jnp.zeros((120, HR), F32)], axis=0)
        stat[...] = total.T * (1.0 / D)
        yc = lanes(y * Dy, Dy)
        gain = vector(0, yc)

        def step(i):
            lr = rows16(i * 16, 16)
            gr = rows16(s * R + c * HR + i * 16, 16)
            mu, inv = stats(tokF[gr, :].astype(F32))
            xhat = (tokF[gr, yc].astype(F32) - mu) * inv
            t = ebuf[s, lr, :] * gain
            st = stat[lr, :]
            m1, m2 = st[:, 0:1], st[:, 1:2]
            g = hid[rows16(s * HR + i * 16, 16), yc]
            ebuf[s, lr, :] = g + inv * (t - m1 - xhat * m2)
        loop(HR // 16, step)
        give_out(s, ebuf, ig, "ig")

    G = [r[f"G{p}"] for p in range(4)]
    RX = [r[f"RX{p}"] for p in range(4)]
    ZL = [r[f"ZL{p}"] for p in range(4)]
    ZR = [r[f"ZR{p}"] for p in range(4)]
    outs = [r[f"o{p}"] for p in range(4)]

    def weight_grad(p, x, g):
        def step(i):
            rr = pl.ds(pl.multiple_of(i * 256, 256), 256)
            G[p][rr, :] = dot_tn(x[:, lanes(i * 256, 256)], g[...]).astype(BF)
        loop(D // 256, step)

    def gblock(p, blk):
        return rows16(blk * RB, RB)

    def rs_cross(p):
        for db in range(1, B):
            bd = lax.rem(b + db, B)
            for aa in range(A):
                send(rcopy(
                    G[p].at[gblock(p, aa * B + bd)], RX[p].at[db - 1, aa],
                    z.rs_x[p] + (db - 1) * A + aa, b_dev(db),
                ))

    def rs_add(p):
        for db in range(1, B):
            for aa in range(A):
                dst = RX[p].at[db - 1, aa]
                rcopy(dst, dst, z.rs_x[p] + (db - 1) * A + aa, mate).wait_recv()
        if B > 1:
            def step(aa):
                rr = gblock(p, aa * B + b)
                total = G[p][rr, :].astype(F32)
                for db in range(B - 1):
                    total = total + RX[p][db, aa].astype(F32)
                G[p][rr, :] = total.astype(BF)
            loop(A, step)

    def rs_line(p, n):
        def pass_on(dest, came, buf, sem, to, go):
            rr = gblock(p, dest * B + b)

            def add():
                dst = buf.at[n]
                rcopy(dst, dst, sem + n, mate).wait_recv()
                G[p][rr, :] = (G[p][rr, :].astype(F32) + buf[n].astype(F32)).astype(BF)
            when(go & came, add)
            send(rcopy(G[p].at[rr], buf.at[n], sem + n, to), go)
        dest = A - 1 - n
        pass_on(dest, a > 0, ZL[p], z.rs_r[p], right, a < dest)
        pass_on(n, a < A - 1, ZR[p], z.rs_l[p], left, a > n)

    def rs_done(p):
        outs[p][...] = G[p][gblock(p, dpi), :].astype(F32)

        def take(buf, sem, n):
            dst = buf.at[n]
            rcopy(dst, dst, sem + n, mate).wait_recv()
            outs[p][...] += buf[n].astype(F32)
        when(a > 0, lambda: take(ZL[p], z.rs_r[p], jnp.clip(A - 1 - a, 0, A - 2)))
        when(a < A - 1, lambda: take(ZR[p], z.rs_l[p], jnp.clip(a, 0, A - 2)))

    def rs_ticks(p):
        ticks.append(functools.partial(rs_add, p))
        for n in range(A - 1):
            ticks.append(functools.partial(rs_line, p, n))
        ticks.append(functools.partial(rs_done, p))

    for s in range(NS):
        project(s)
        tick(1)
        loop(z.NP, functools.partial(attend, s))
        tick(3 if s == 0 else 1)
        core_part(s, "branch", att, W[1], cr1)
        chip_part(s, "branch", att, W[1], cr1, yr1)
    rows_relay(1)
    rows_done(1)
    tick(1)
    while len(ticks) > A + 1:
        tick()
    tick(1)
    for s in range(NS):
        norm_two(s)
        tick(1)
        up(s)
    while ticks:
        tick()
    for s in range(NS):
        back_up(s)
        core_part(s, "gn2", gp, W[2], cr2)
    for s in range(NS):
        chip_part(s, "gn2", gp, W[2], cr2, yr2)
    weight_grad(3, feedF, na_act)
    rs_cross(3)
    weight_grad(2, n2, gp)
    rs_cross(2)
    rs_ticks(3)
    rs_ticks(2)
    gvl[...] = jnp.zeros_like(gvl)
    ones_row = jnp.ones((8, z.ROWS), BF)
    gvl[5:6, lanes(mpi * Dm, Dm)] = dot(ones_row, r["feed"][...])[0:1]
    gvl[6:7, 0:F] = dot(ones_row, gp[...])[0:1]
    for s in range(NS):
        core_part(s, "out", na_act, W[3], cr1)
    for s in range(NS):
        norm_two_back(s)
        chip_share(s, "out", na_act, W[3], cr1, yrO)
        tick(1)
        attend_back_start(s)
        tick(1)
        loop(z.NP, functools.partial(attend_back, s))
        tick(1)
        core_part(s, "gn1", gj, W[0], cr3)
        tick(1)
        chip_share(s, "gn1", gj, W[0], cr3, yr3)
    for s in range(NS):
        layer_out(s)
    norm_one()
    weight_grad(0, na.at[:, 0:D], gj)
    rs_cross(0)
    weight_grad(1, gb, att)
    rs_cross(1)
    rs_ticks(0)
    rs_ticks(1)
    gvl[7:8, 0:HW] = dot(ones_row, gj[:, 0:HW])[0:1]
    gvl[7:8, HW:2 * HW] = dot(ones_row, gj[:, 2 * HW:3 * HW])[0:1]
    yc = lanes(y * Dy, Dy)
    for row, i in ((3, 0), (4, 1), (2, 2)):
        gvl[row:row + 1, yc] = jnp.sum(acc[i, :, yc], axis=0, keepdims=True)
    for s in range(NS):
        norm_one_sums(s)
        tick(1)
    for s in range(NS):
        norm_one_back(s)
        tick(1)
    vst[1, 0] = gvl[...]
    vec_send(1, 0)
    tick(2)
    vec_add(1, 0)
    vec_send(1, 1)
    tick(1)
    vec_add(1, 1)
    vec_send(1, 2)
    tick(1)
    vec_add(1, 2)
    vec_send(1, 3)
    tick(1)
    vec_add(1, 3)
    r["gvec"][...] = vst[1, 4]
    while ticks:
        tick()
    for s in range(NS):
        take_out(s, lo, "lo")
        take_out(s, ig, "ig")
    for key in list(busy):
        free(key)
    for cond, copy in pending:
        when(cond, lambda copy=copy: copy.wait_send())


def body(mesh, tokens, slot_flags, cotangent, attend_gain, attend_shift, input_weight, input_bias,
         output_weight, output_bias, dense_gain, dense_shift, up_weight, up_bias, down_weight, down_bias):
    z = Sizes(mesh, tokens, input_weight, up_weight)
    dpi, mpi = lax.axis_index("dp"), lax.axis_index("mp")
    filled = slot_flags.astype(F32)[:, None, None]
    pad = ((0, 0), (0, z.R - z.SEQ), (0, 0))
    tok = jnp.pad(tokens, pad).reshape(z.ROWS, z.Dm)
    feed = jnp.pad((cotangent.astype(F32) * filled).astype(BF), pad).reshape(z.ROWS, z.Dm)
    hot_dp = (jnp.arange(z.dp) == dpi).astype(F32)
    hot_mp = (jnp.arange(z.mp) == mpi).astype(F32)
    wide = jnp.stack([attend_gain, attend_shift, output_bias, dense_gain, dense_shift, down_bias]).astype(F32)
    wide = wide[:, None, :, None, :] * hot_mp[:, None, None, None] * hot_dp[:, None]
    wide = wide.reshape(6, z.D)
    up_row = (up_bias.astype(F32)[:, None, :] * hot_dp[:, None]).reshape(1, z.F)
    in_row = (input_bias.astype(F32)[:, :, None, :] * hot_dp[:, None]).reshape(1, 2 * z.HW)
    rows = [jnp.pad(row, ((0, 0), (0, z.VW - row.shape[1]))) for row in (wide, up_row, in_row)]
    vec = jnp.concatenate(rows, axis=0)
    shapes = [
        jax.ShapeDtypeStruct((z.ROWS, z.Dm), BF),
        jax.ShapeDtypeStruct((z.ROWS, z.Dm), F32),
    ] + [jax.ShapeDtypeStruct((z.RB, n), F32) for n in z.cols] + [jax.ShapeDtypeStruct((8, z.VW), F32)]
    vmem = pl.BlockSpec(memory_space=pltpu.VMEM)
    lo, ig, g0, g1, g2, g3, gvec = pl.pallas_call(
        functools.partial(kernel, z),
        out_shape=shapes,
        in_specs=[vmem] * 7,
        out_specs=[vmem] * 7,
        scratch_shapes=scratch_shapes(z),
        compiler_params=pltpu.CompilerParams(
            collective_id=0, has_side_effects=True, vmem_limit_bytes=VMEM_LIMIT
        ),
        name="layer",
    )(
        tok, feed, input_weight.reshape(z.RB, 3 * z.HW), output_weight.T, up_weight, down_weight.T, vec
    )

    def own_part(row):
        part = row.reshape(z.mp, -1, z.dp, HD // z.dp)
        part = lax.dynamic_index_in_dim(part, mpi, 0, keepdims=False)
        return lax.dynamic_index_in_dim(part, dpi, 1, keepdims=False)

    def dp_part(row):
        part = row.reshape(-1, z.dp, HD // z.dp)
        return lax.dynamic_index_in_dim(part, dpi, 1, keepdims=False)

    layer_rows = (lo.reshape(z.NS, z.R, z.Dm)[:, :z.SEQ].astype(F32) * filled).astype(BF)
    input_grad = ig.reshape(z.NS, z.R, z.Dm)[:, :z.SEQ]
    d_rows = gvec[:6, :z.D]
    return (
        layer_rows,
        input_grad,
        own_part(d_rows[0]),
        own_part(d_rows[1]),
        g0.reshape(input_weight.shape),
        dp_part(gvec[7, :2 * z.HW]).reshape(input_bias.shape),
        g1.T,
        own_part(d_rows[2]),
        own_part(d_rows[3]),
        own_part(d_rows[4]),
        g2,
        dp_part(gvec[6, :z.F]),
        g3.T,
        own_part(d_rows[5]),
    )


VMEM_LIMIT = 63 * 2**20


def solution(mesh):
    rows = P("dp", None, "mp")
    vec = P("mp", "dp")
    pair = P(None, "mp", "dp")
    return jax.shard_map(
        functools.partial(body, mesh),
        mesh=mesh,
        in_specs=(rows, P("dp"), rows, vec, vec, rows, pair, vec, vec, vec, vec, P("dp", "mp"), vec, vec, vec),
        out_specs=(rows, rows, vec, vec, rows, pair, vec, vec, vec, vec, P("dp", "mp"), vec, vec, vec),
        check_vma=False,
    )
```

time: 1160 us -> 296 us (0.26)
  blocking collectives: 480 us -> 0 us
  waiting for transfers between devices: 423 us -> 0 us
  Pallas kernels: 0 us -> 270 us
  matrix products: 131 us -> 0 us
  other arithmetic: 54.6 us -> 2.75 us
  local copies, waits for them, and re-layouts: 53.9 us -> 21.6 us
  between operations: 16.7 us -> 0.93 us
    all_gather x18 -> x0, blocking collectives: 395 us -> none  [the longest x2 61 us: slot_step(): lax.all_gather(input_bias, 'dp', axis=2, tiled=True)]
    pallas_call x0 -> x1, Pallas kernels: none -> 270 us  [body(): pl.pallas_call(functools.partial(kernel, z), out_shape=shapes, in_specs=[...]
    reduce_scatter x10 -> x0, waiting for transfers between devices: 198 us -> none  [the longest x1 68.3 us: body(): lax.psum_scatter(running[8].astype(jnp.bfloat16), 'dp', scatter_dimension...]
    all_gather x14 -> x0, waiting for transfers between devices: 144 us -> none  [the longest x2 107 us: slot_step(): lax.all_gather(down_weight, 'dp', axis=1, tiled=True)]
    dot_general x36 -> x0, matrix products: 131 us -> none  [the longest x6 30.2 us: product(): return jnp.dot(left_side, right_side, preferred_element_type=jnp.float32)]
    unnamed x6 -> x0, waiting for transfers between devices: 76.9 us -> none
    psum x8 -> x0, blocking collectives: 47.2 us -> none  [the longest x4 23.8 us: normalize(): lax.psum((jnp.sum(values, axis=1), jnp.sum(values * values, axis=1)), 'mp')]
    unnamed x1 -> x0, blocking collectives: 37.4 us -> none
  transfers between devices with their start and end apart: 26 -> 0, of which waited for: 16 -> 0; matrix products, arithmetic and copies ran while one was open for 13% -> 0% of each run, Pallas kernels for 0% -> 0%
where the time goes in v1:
time: 296 us; the launch traced here: 295 us
  Pallas kernels  270 us (91%)
  local copies, waits for them, and re-layouts  21.6 us (7%)
    pallas_call x1, Pallas kernels, body(): pl.pallas_call(functools.partial(kernel, z), out_shape=shapes, in_specs=[...  270 us
    unnamed x41, local copies, waits for them, and re-layouts  10.6 us

profile of v1, /device:TPU:0, one launch (start us, length us, event | category | flops | bytes accessed | tf_op | source)
XLA Modules:
  0.0 295.1 jit_solution(17575309916011080333)
XLA Ops:
  0.6 0.0 copy-start.10
  0.7 0.0 copy-start.11
  0.7 0.0 copy-start.12
  0.7 0.0 copy-start.1
  0.7 0.1 mul.105
  0.8 0.1 mul.106
  0.9 0.7 constant_dynamic-update-slice_fusion.5
  1.6 0.7 constant_dynamic-update-slice_fusion.4
  2.3 0.7 constant_dynamic-update-slice_fusion.3
  2.9 0.7 constant_dynamic-update-slice_fusion.2
  3.6 0.7 constant_dynamic-update-slice_fusion.1
  4.3 0.7 constant_dynamic-update-slice_fusion
  5.0 0.1 broadcast_multiply_fusion.1
  5.1 0.2 mul.104
  5.4 0.0 copy-done.10
  5.4 0.1 copy.53
  5.5 0.1 broadcast_multiply_fusion
  5.5 0.1 mul.112
  5.6 0.0 copy-done.11
  5.7 0.1 broadcast_multiply_fusion.2
  5.7 0.1 mul.116
  5.8 0.6 select_maximum_fusion.refs_6_
  6.5 0.5 multiply_convert_fusion.1
  7.0 0.0 copy-start.2
  7.0 0.1 copy.79
  7.1 0.9 pad.12.clone
  8.0 0.1 copy-done.2
  8.1 0.1 copy.78
  8.2 0.0 copy-start.6
  8.2 0.0 copy-start.9
  8.2 0.9 pad.11.clone
  9.1 0.2 copy.50
  9.2 0.8 copy.54.refs_2_
  10.1 0.0 copy-done.6
  10.1 0.8 copy.52
  10.9 0.7 copy.51
  11.7 269.9 %layer.1 = (bf16[1216,256]{1,0:T(8,128)(2,1)}, f32[1216,256]{1,0:T(8,128)}, f32[128,768]{1,0:T(8,128)}, f32[128,256]{1,0:T(8,128)}, f32[128,1024]{1,0:T(8,128)}, /*index=5*/f32[128,1024]{1,0:T(8,128)}, f32[8,1024]{1,0:T(8,128)}) custom-call(bf16[1216,256]{1,0:T(8,128)(2,1)} %bitcast.51, bf16[1216,256]{1,0:T(8,128)(2,1)} %bitcast.50, ...), custom_call_target="tpu_custom_call" | custom-call | tf_op jit(solution)/shard_map/layer/pallas_call | solution.py:866
  281.6 1.1 slice_reduce_fusion
  282.7 0.1 reshape_squeeze.29
  282.8 0.1 reshape_squeeze.31
  282.9 0.6 constant_dynamic-slice_fusion
  283.5 0.1 reshape_squeeze.27
  283.6 0.1 reshape_squeeze.28
  283.6 0.6 constant_dynamic-slice_fusion.3
  284.2 0.1 reshape_squeeze.24
  284.3 0.1 reshape_squeeze.25
  284.4 0.6 constant_dynamic-slice_fusion.6
  285.0 0.1 reshape_squeeze.30
  285.1 0.7 copy.64
  285.8 0.7 slice_reduce_fusion.7
  286.5 0.1 reshape_squeeze.26
  286.6 0.6 constant_dynamic-slice_fusion.5
  287.2 1.2 slice.47
  288.4 1.3 multiply_convert_fusion
  289.8 0.0 copy-done
  289.8 0.1 slice.48
  289.9 1.6 copy.70
  291.5 0.2 copy.59
  291.7 0.0 copy-start.3
  291.7 0.9 copy.66
  292.6 0.0 copy-done.4
  292.6 1.0 copy.68
  293.6 0.8 copy.67
  294.3 0.8 copy.87
  (20 shorter events, 0.1 us)
Async XLA Ops:
  0.6 4.7 %copy-start.10 = (bf16[16,8]{0,1:T(8,128)(2,1)S(1)}, bf16[16,8]{0,1:T(8,128)(2,1)}, u32[]{:S(2)}) copy-start(bf16[16,8]{0,1:T(8,128)(2,1)} %param.27) | copy-start | bytes 772
  0.7 5.0 %copy-start.11 = (bf16[2,4,8]{2,1,0:T(4,128)(2,1)S(1)}, bf16[2,4,8]{2,1,0:T(4,128)(2,1)}, u32[]{:S(2)}) copy-start(bf16[2,4,8]{2,1,0:T(4,128)(2,1)} %param.21) | copy-start | bytes 388
  0.7 5.8 %copy-start.12 = (s32[2]{0:T(128)S(1)}, s32[2]{0:T(128)}, u32[]{:S(2)}) copy-start(s32[2]{0:T(128)} %param.16) | copy-start | bytes 28
  0.7 5.8 %copy-start.1 = (bf16[2,577,256]{2,0,1:T(2,128)(2,1)S(1)}, bf16[2,577,256]{2,0,1:T(2,128)(2,1)}, u32[]{:S(2)}) copy-start(bf16[2,577,256]{2,0,1:T(2,128)(2,1)} %param.17) | copy-start | bytes 1772548
  7.0 1.1 copy-start.2
  8.1 1.0 copy-start.7
  8.2 1.9 copy-start.6
  8.2 2.7 copy-start.9
  287.2 2.6 copy-start
  289.9 1.6 copy-start.5
  291.5 1.1 copy-start.4
  291.5 2.1 copy-start.8
  291.7 2.7 copy-start.3
